TPU v7x, 32 devices: a whole 2x2x4 slice. The times are simulated.
32 devices in a mesh: groups: 2 (over y), tiles: 4 (over z), rows: 2 (over x), tok: 2 (over core).
Axes of the slice: x: 2, y: 2, z: 4, core: 2. Of those that a mesh axis runs over, the one named last changes fastest.
Arguments:
- x_act: bfloat16 [2, 1536, 8192], P('tok', 'groups', 'rows'), parts along dimension 1, may hold values from -6 to 6
- grad_out: bfloat16 [2, 1536, 28672], P('tok', 'groups', ('tiles', 'rows')), parts along dimension 1, may hold values from -0.21875 to 0.21875
- surv_rows: int32 [8, 2, 64], P(('groups', 'tiles'), 'rows'), parts along dimension 0, may hold values from 0 to 31, as said below
- surv_cols: int32 [8, 2, 64], P(('groups', 'tiles'), 'rows'), parts along dimension 0, may hold values from 0 to 55, as said below
- counts: int32 [8, 2], P(('groups', 'tiles'), 'rows'), parts along dimension 0, may hold values from 16 to 64, as said below
Outputs:
- fisher: float32 [8, 2, 64, 128, 128], P(('groups', 'tiles'), 'rows', None, 'tok'), parts along dimension 0
There are 2 independent parts, one for each index of `groups`. A program takes and returns all parts, laid end to end along the dimension named above; each array names one. Nothing has to cross between parts.
Inputs may be any that keep to these rules, and one draw needn't show every extreme that they name: `surv_rows`: the (row tile, column tile) pairs listed in one device's slots are distinct. `surv_cols`: same slots as surv_rows. A device's survivors occupy its slots 0 to counts - 1; in every draw some device lists 64.
All inputs are finite; a program needn't handle non-finite values.
Results may differ from a plain program's by a relative error of at most 0.0003.
Values may be sent and summed in bfloat16 or wider, within the bound.
A program may use at most 128 MiB of HBM per device.

v0:
```python
import jax
import jax.numpy as jnp
from jax import lax
from jax.sharding import PartitionSpec as P

TILE = 128


def square_tiles(x_tiles, panel_fetch, row_index, live_count, places, slot_total):
    tile_extent = x_tiles.shape[2]
    block_size = min(16, slot_total)
    result = jnp.zeros((slot_total, tile_extent, tile_extent), jnp.float32)

    def one_block(block_index, totals):
        first_slot = block_index * block_size
        rows_here = lax.dynamic_slice_in_dim(row_index, first_slot, block_size)
        x_panels = jnp.take(x_tiles, rows_here, axis=1)
        y_panels = panel_fetch(first_slot, block_size)
        gradients = jnp.einsum(
            "tnk,tnj->nkj", x_panels, y_panels, preferred_element_type=jnp.float32
        )
        is_live = first_slot + jnp.arange(block_size, dtype=jnp.int32) < live_count
        squares = jnp.where(is_live[:, None, None], gradients * gradients, 0.0)
        where_to = lax.dynamic_slice_in_dim(places, first_slot, block_size)
        return totals.at[where_to].set(squares)

    trip_count = (live_count + block_size - 1) // block_size
    return lax.fori_loop(0, trip_count, one_block, result)


def sum_samples(partial_value):
    return lax.psum_scatter(partial_value, "tok", scatter_dimension=1, tiled=True)


def on_device(x_act, grad_out, surv_rows, surv_cols, counts):
    tile_extent = TILE
    gathered = lax.all_gather(grad_out, "rows", axis=2, tiled=True)
    length_value = x_act.shape[1]
    x_tiles = x_act[0].reshape(length_value, -1, tile_extent)
    y_tiles = gathered[0].reshape(length_value, -1, tile_extent)
    row_listing = surv_rows[0, 0]
    cols_list = surv_cols[0, 0]
    live_here = counts[0, 0]
    capacity = row_listing.shape[0]
    keep_count = capacity // 2

    def from_own(first_slot, block_size):
        cols_here = lax.dynamic_slice_in_dim(cols_list, first_slot, block_size)
        return jnp.take(y_tiles, cols_here, axis=1)

    owners = lax.axis_size("tiles")
    position = lax.axis_index("tiles")
    deal_size = (capacity - keep_count) // owners
    own_places = jnp.arange(keep_count, dtype=jnp.int32)
    own_part = square_tiles(
        x_tiles,
        from_own,
        row_listing[:keep_count],
        jnp.minimum(live_here, keep_count),
        own_places,
        keep_count,
    )
    outbound_tiles = jnp.take(y_tiles, cols_list[keep_count:], axis=1)
    outbound_tiles = outbound_tiles.reshape(length_value, owners, deal_size, tile_extent)
    outbound_tiles = jnp.roll(outbound_tiles, position, axis=1).reshape(
        length_value, owners * deal_size, tile_extent
    )
    incoming = lax.all_to_all(outbound_tiles, "tiles", split_axis=1, concat_axis=1, tiled=True)
    all_rows, all_counts = (
        lax.all_gather(surv_rows, "tiles", axis=0, tiled=True),
        lax.all_gather(counts, "tiles", axis=0, tiled=True),
    )
    sources = jnp.arange(owners, dtype=jnp.int32)
    block_of = (position - sources) % owners
    slot_ids = (
        keep_count + block_of[:, None] * deal_size + jnp.arange(deal_size, dtype=jnp.int32)[None, :]
    )
    wanted_rows = jnp.take_along_axis(all_rows[:, 0, :], slot_ids, axis=1).reshape(-1)
    is_wanted = (slot_ids < all_counts[:, 0][:, None]).reshape(-1)
    ordering = jnp.argsort(1 - is_wanted.astype(jnp.int32), stable=True)
    wanted_total = jnp.sum(is_wanted.astype(jnp.int32))

    def from_incoming(first_slot, block_size):
        picks = lax.dynamic_slice_in_dim(ordering, first_slot, block_size)
        return jnp.take(incoming, picks, axis=1)

    helped = square_tiles(
        x_tiles, from_incoming, wanted_rows[ordering], wanted_total, ordering, owners * deal_size
    )
    returned_tiles = lax.all_to_all(helped, "tiles", split_axis=0, concat_axis=0, tiled=True)
    returned_tiles = returned_tiles.reshape(owners, deal_size, tile_extent, tile_extent)
    returned_tiles = jnp.roll(returned_tiles, -position, axis=0).reshape(
        owners * deal_size, tile_extent, tile_extent
    )
    fisher = sum_samples(jnp.concatenate([own_part, returned_tiles], axis=0))
    return fisher[None, None]


def solution(mesh):
    return jax.shard_map(
        on_device,
        mesh=mesh,
        in_specs=(
            P("tok", "groups", "rows"),
            P("tok", "groups", ("tiles", "rows")),
            P(("groups", "tiles"), "rows", None),
            P(("groups", "tiles"), "rows", None),
            P(("groups", "tiles"), "rows"),
        ),
        out_specs=P(("groups", "tiles"), "rows", None, "tok", None),
        check_vma=False,
    )
```

profile of v0, /device:TPU:0, one launch (start us, length us, event | category | flops | bytes accessed | tf_op | source)
XLA Modules:
  0.0 466.5 jit_solution(16926577324850607619)
XLA Ops:
  6.5 8.3 %copy.25 = bf16[1,768,3584]{1,2,0:T(8,128)(2,1)} copy(bf16[1,768,3584]{2,1,0:T(8,128)(2,1)} %param.12) | data formatting | bytes 11010048 | tf_op args[1]
  15.7 137.3 %all-gather.2.cloned.1.call-done = bf16[1,768,7168]{1,2,0:T(8,128)(2,1)} async-done(((bf16[1,768,3584]{1,2,0:T(8,128)(2,1)}), bf16[1,768,7168]{1,2,0:T(8,128)(2,1)}) %all-gather.2.cloned.1.call-update) | async-done | bytes 11010064 | tf_op jit(solution)/shard_map/all_gather | solution.py:37
  153.0 14.7 %copy.27 = bf16[768,56,128]{2,0,1:T(8,128)(2,1)} copy(bf16[768,56,128]{0,2,1:T(8,128)(2,1)} %bitcast.65) | data formatting | bytes 22020096 | tf_op jit(solution)/shard_map/while | solution.py:28
  167.7 8.1 %gather_fusion.5 = bf16[32,768,128]{2,1,0:T(8,128)(2,1)} fusion(bf16[768,56,128]{2,0,1:T(8,128)(2,1)} %copy.27, s32[1024]{0:T(1024)S(1)} %pad_clamp_fusion.4), kind=kCustom, calls=%fused_computation.5 | custom fusion | bytes 12583040 | tf_op jit(solution)/shard_map/jit(_take)/gather | solution.py:63
  183.5 5.4 %all-to-all-start = ((bf16[768,32,128]{2,0,1:T(8,128)(2,1)}), bf16[768,32,128]{2,0,1:T(8,128)(2,1)}, u32[]{:S(2)}, u32[]{:S(2)}) async-start(bf16[768,32,128]{2,0,1:T(8,128)(2,1)} %bitcast.62), calls=%async_computation | async-start | bytes 12582912 | tf_op jit(solution)/shard_map/all_to_all | solution.py:68
  190.8 136.6 %all-reduce = s32[4]{0:T(128)S(1)} all-reduce(s32[4]{0:T(128)S(1)} %bitcast_dynamic-update-slice_fusion), channel_id=1, replica_groups=mesh['groups'=2,'tiles'=4,'rows'=2,'tok'=2] {'tiles'}, use_global_device_ids=true, to_apply=%add | all-reduce | flops 4 | bytes 32
  329.4 8.6 %copy.24 = bf16[1,768,4096]{1,2,0:T(8,128)(2,1)} copy(bf16[1,768,4096]{2,1,0:T(8,128)(2,1)} %param.11) | data formatting | bytes 12582912 | tf_op args[0]
  338.0 8.6 %copy.26 = bf16[768,32,128]{2,0,1:T(8,128)(2,1)} copy(bf16[768,32,128]{0,2,1:T(8,128)(2,1)} %bitcast.64) | data formatting | bytes 12582912 | tf_op jit(solution)/shard_map/while | solution.py:28
  346.7 9.0 %all_gather.11 = s32[4,1,64]{2,1,0:T(1,128)S(1)} all-gather(s32[1,1,64]{2,1,0:T(1,128)S(1)} %copy-done.2), channel_id=1, replica_groups=mesh['groups'=2,'tiles'=4,'rows'=2,'tok'=2] {'tiles'}, dimensions={0}, use_global_device_ids=true | all-gather | bytes 1280 | tf_op jit(solution)/shard_map/all_gather | solution.py:70
  360.3 35.5 %while.21 = (s32[]{:T(128)}, f32[32,128,128]{2,1,0:T(8,128)}, s32[]{:T(128)}, s32[32]{0:T(128)S(1)}, s32[]{:T(128)}, /*index=5*/s32[32]{0:T(128)S(1)}, bf16[768,...) while((s32[]{:T(128)}, f32[32,128,128]{2,1,0:T(8,128)}, ...), condition=%wide.region_7.9_spmd, body=%wide.region_5.8_spmd.sunk | while | flops 406325472 | bytes 23077720 | solution.py:28
  364.3 5.4 %gather_fusion.3 = bf16[16,768,128]{2,1,0:T(8,128)(2,1)} fusion(bf16[768,32,128]{2,0,1:T(8,128)(2,1)} %get-tuple-element.335, s32[1024]{0:T(1024)S(1)} %pad_clamp_fusion.13), kind=kCustom, calls=%fused_computation.2.clone.clone.1 | custom fusion | bytes 6291520 | tf_op jit(solution)/shard_map/while/body/jit(_take)/gather | solution.py:17
  370.4 4.3 fusion.59
  382.1 5.4 %gather_fusion.3 = bf16[16,768,128]{2,1,0:T(8,128)(2,1)} fusion(bf16[768,32,128]{2,0,1:T(8,128)(2,1)} %get-tuple-element.335, s32[1024]{0:T(1024)S(1)} %pad_clamp_fusion.13), kind=kCustom, calls=%fused_computation.2.clone.clone.1 | custom fusion | bytes 6291520 | tf_op jit(solution)/shard_map/while/body/jit(_take)/gather | solution.py:17
  388.1 4.3 fusion.59
  395.8 4.5 all-to-all-start.1
  401.9 37.3 %while.20 = (s32[]{:T(128)}, f32[32,128,128]{2,1,0:T(8,128)}, s32[]{:T(128)}, s32[32]{0:T(128)S(1)}, s32[]{:T(128)}, /*index=5*/s32[32]{0:T(128)S(1)}, bf16[768,...) while((s32[]{:T(128)}, f32[32,128,128]{2,1,0:T(8,128)}, ...), condition=%wide.region_2.4_spmd, body=%wide.region_0.3_spmd.sunk | while | flops 406325536 | bytes 23077896 | solution.py:28
  402.1 5.3 %gather_fusion = bf16[16,768,128]{2,1,0:T(8,128)(2,1)S(1)} fusion(bf16[768,56,128]{2,0,1:T(8,128)(2,1)} %get-tuple-element.377, s32[1024]{0:T(1024)S(1)} %pad_clamp_fusion.10), kind=kCustom, calls=%fused_computation.1.clone.1 | custom fusion | bytes 6291520 | tf_op jit(solution)/shard_map/while/body/jit(_take)/gather | solution.py:49
  407.4 5.4 %gather_fusion.1 = bf16[16,768,128]{2,1,0:T(8,128)(2,1)} fusion(bf16[768,32,128]{2,0,1:T(8,128)(2,1)} %get-tuple-element.375, s32[1024]{0:T(1024)S(1)} %pad_clamp_fusion.11), kind=kCustom, calls=%fused_computation.clone.clone.1 | custom fusion | bytes 6291520 | tf_op jit(solution)/shard_map/while/body/jit(_take)/gather | solution.py:17
  412.8 4.4 fusion.56
  420.7 5.3 %gather_fusion = bf16[16,768,128]{2,1,0:T(8,128)(2,1)S(1)} fusion(bf16[768,56,128]{2,0,1:T(8,128)(2,1)} %get-tuple-element.377, s32[1024]{0:T(1024)S(1)} %pad_clamp_fusion.10), kind=kCustom, calls=%fused_computation.1.clone.1 | custom fusion | bytes 6291520 | tf_op jit(solution)/shard_map/while/body/jit(_take)/gather | solution.py:49
  426.0 5.4 %gather_fusion.1 = bf16[16,768,128]{2,1,0:T(8,128)(2,1)} fusion(bf16[768,32,128]{2,0,1:T(8,128)(2,1)} %get-tuple-element.375, s32[1024]{0:T(1024)S(1)} %pad_clamp_fusion.11), kind=kCustom, calls=%fused_computation.clone.clone.1 | custom fusion | bytes 6291520 | tf_op jit(solution)/shard_map/while/body/jit(_take)/gather | solution.py:17
  431.4 4.4 fusion.56
  439.2 6.8 %all-to-all-done.1 = f32[32,128,128]{2,1,0:T(8,128)} async-done(((f32[32,128,128]{2,1,0:T(8,128)}), f32[32,128,128]{2,1,0:T(8,128)}, u32[]{:S(2)}, u32[]{:S(2)}) %all-to-all-start.1) | async-done | bytes 2097184 | tf_op jit(solution)/shard_map/all_to_all | solution.py:90
  450.3 9.4 %reduce-scatter.2.cloned.1.call-done = f32[64,64,128]{2,1,0:T(8,128)} async-done(((f32[64,128,128]{2,1,0:T(8,128)}), f32[64,64,128]{2,1,0:T(8,128)}) %reduce-scatter.2.cloned.1.call-update) | async-done | bytes 2097168 | tf_op jit(solution)/shard_map/reduce_scatter | solution.py:32
  (72 shorter events, 44.8 us)
Async XLA Ops:
  6.5 146.5 %all-gather.2.cloned.1.call-start = ((), (), s32[]{:S(2)}) async-start(), calls=%async_computation.3 | async-start | bytes 16515072 | tf_op jit(solution)/shard_map/all_gather | solution.py:37
  14.8 0.7 copy-start.1
  183.5 6.1 %copy-start.3 = (u32[32]{0:T(128)S(1)}, u32[32]{0:T(128)}, u32[]{:S(2)}) copy-start(u32[32]{0:T(128)} %constant.189) | copy-start | bytes 388
  183.5 175.3 %all-to-all-start = ((bf16[768,32,128]{2,0,1:T(8,128)(2,1)}), bf16[768,32,128]{2,0,1:T(8,128)(2,1)}, u32[]{:S(2)}, u32[]{:S(2)}) async-start(bf16[768,32,128]{2,0,1:T(8,128)(2,1)} %bitcast.62), calls=%async_computation | async-start | bytes 12582912 | tf_op jit(solution)/shard_map/all_to_all | solution.py:68
  338.0 8.6 %copy-start.2 = (s32[1,1,64]{2,1,0:T(1,128)S(1)}, s32[1,1,64]{2,1,0:T(1,128)}, u32[]{:S(2)}) copy-start(s32[1,1,64]{2,1,0:T(1,128)} %param.13) | copy-start | bytes 772
  395.8 50.2 %all-to-all-start.1 = ((f32[32,128,128]{2,1,0:T(8,128)}), f32[32,128,128]{2,1,0:T(8,128)}, u32[]{:S(2)}, u32[]{:S(2)}) async-start(f32[32,128,128]{2,1,0:T(8,128)} %get-tuple-element.100), calls=%async_computation.1 | async-start | bytes 4194304 | tf_op jit(solution)/shard_map/all_to_all | solution.py:90
  400.3 59.4 %reduce-scatter.2.cloned.1.call-start = ((), (), s32[]{:S(2)}) async-start(), calls=%async_computation.4 | async-start | bytes 6291456 | tf_op jit(solution)/shard_map/reduce_scatter | solution.py:32
  439.2 8.7 %copy-start = (f32[32,128,128]{2,1,0:T(8,128)S(1)}, f32[32,128,128]{2,1,0:T(8,128)}, u32[]{:S(2)}) copy-start(f32[32,128,128]{2,1,0:T(8,128)} %get-tuple-element.98) | copy-start | bytes 6291460
Sparse Core Ops, SparseCore 0:
  15.0 137.9 all-gather.1
  450.4 9.2 reduce-scatter.1
where the time goes:
time: 469 us; the launch traced here: 467 us
  waiting for transfers between devices  153 us (33%)
  blocking collectives  146 us (31%)
  local copies, waits for them, and re-layouts  109 us (23%)
  matrix products  17.4 us (4%)
  other arithmetic  16.1 us (3%)
  between operations  14.8 us (3%)
  starting transfers between devices  9.92 us (2%)
    all_gather x1, waiting for transfers between devices, on_device(): gathered = lax.all_gather(grad_out, 'rows', axis=2, tiled=True)  137 us
    unnamed x1, blocking collectives  137 us
    while x2, local copies, waits for them, and re-layouts, square_tiles(): return lax.fori_loop(0, trip_count, one_block, result)  23.3 us
    gather x4, local copies, waits for them, and re-layouts, one_block(): x_panels = jnp.take(x_tiles, rows_here, axis=1)  21.6 us
    unnamed x12, local copies, waits for them, and re-layouts  18.8 us
    dot_general x4, matrix products, one_block(): jnp.einsum('tnk,tnj->nkj', x_panels, y_panels, preferred_element_type=jnp...  17.4 us
    scatter x4, local copies, waits for them, and re-layouts, one_block(): return totals.at[where_to].set(squares)  13.5 us
    gather x2, local copies, waits for them, and re-layouts, from_own(): return jnp.take(y_tiles, cols_here, axis=1)  10.6 us
  transfers between devices with their start and end apart: 4, of which 3 were waited for; matrix products, arithmetic and copies ran while one was open for 13% of the time, Pallas kernels for 0%

commit v1 on v0

--- a/solution.py
+++ b/solution.py
@@ -1,6 +1,10 @@
+import functools
+
 import jax
 import jax.numpy as jnp
 from jax import lax
+from jax.experimental import pallas as pl
+from jax.experimental.pallas import tpu as pltpu
 from jax.sharding import PartitionSpec as P
 
 TILE = 128
@@ -96,9 +100,211 @@
     return fisher[None, None]
 
 
+def pack_body(pick_ref, y_ref, out_ref):
+    out_ref[...] = y_ref[...]
+
+
+def pack_panels(y, picks):
+    tokens = y.shape[1]
+    chosen = picks.shape[0]
+    return pl.pallas_call(
+        pack_body,
+        out_shape=jax.ShapeDtypeStruct((chosen, tokens, TILE), y.dtype),
+        grid_spec=pltpu.PrefetchScalarGridSpec(
+            num_scalar_prefetch=1,
+            grid=(chosen,),
+            in_specs=[pl.BlockSpec((1, tokens, TILE), lambda i, p: (0, 0, p[i]))],
+            out_specs=pl.BlockSpec((1, tokens, TILE), lambda i, p: (i, 0, 0)),
+        ),
+        cost_estimate=pl.CostEstimate(
+            flops=0, bytes_accessed=4 * chosen * tokens * TILE, transcendentals=0
+        ),
+        name="pack_panels",
+    )(picks, y)
+
+
+def square_body(apart, steps_ref, rows_ref, cols_ref, slots_ref, x_ref, y_ref, a_ref, b_ref, keep_ref, send_ref):
+    del a_ref, b_ref
+    tokens = x_ref.shape[1]
+    half = TILE // 2
+    first = lax.axis_index("tok") == 0
+
+    def one_slot(x_tile, y_tile, keep_tile, send_tile):
+        gradient = lax.dot_general(
+            x_tile[0], y_tile[0], (((0,), (0,)), ((), ())), preferred_element_type=jnp.float32
+        )
+        squares = gradient * gradient
+
+        @pl.when(first)
+        def _():
+            keep_tile[0] = squares[:half]
+            send_tile[0] = squares[half:]
+
+        @pl.when(jnp.logical_not(first))
+        def _():
+            keep_tile[0] = squares[half:]
+            send_tile[0] = squares[:half]
+
+    y_map = (lambda i: (cols_ref[i], 0, 0)) if apart else (lambda i: (0, 0, cols_ref[i]))
+    out_spec = pl.BlockSpec((1, half, TILE), lambda i: (slots_ref[i], 0, 0))
+    pltpu.emit_pipeline(
+        one_slot,
+        grid=(steps_ref[0],),
+        in_specs=[
+            pl.BlockSpec((1, tokens, TILE), lambda i: (0, 0, rows_ref[i])),
+            pl.BlockSpec((1, tokens, TILE), y_map),
+        ],
+        out_specs=[out_spec, out_spec],
+    )(x_ref, y_ref, keep_ref, send_ref)
+
+
+def square_slots(x, y, steps, rows, cols, slots, keep, send, panels_apart):
+    tokens = x.shape[1]
+    any_spec = pl.BlockSpec(memory_space=pl.ANY)
+    smem_spec = pl.BlockSpec(memory_space=pltpu.SMEM)
+    expected = max(1, rows.shape[0] // (8 if panels_apart else 2))
+    return pl.pallas_call(
+        functools.partial(square_body, panels_apart),
+        out_shape=(
+            jax.ShapeDtypeStruct(keep.shape, keep.dtype),
+            jax.ShapeDtypeStruct(send.shape, send.dtype),
+        ),
+        in_specs=[smem_spec] * 4 + [any_spec] * 4,
+        out_specs=(any_spec, any_spec),
+        input_output_aliases={6: 0, 7: 1},
+        cost_estimate=pl.CostEstimate(
+            flops=expected * 2 * tokens * TILE * TILE,
+            bytes_accessed=expected * (4 * tokens * TILE + 4 * TILE * TILE),
+            transcendentals=0,
+        ),
+        name="square_slots",
+    )(steps.reshape(1), rows, cols, slots, x, y, keep, send)
+
+
+def chunk_sizes(total):
+    last = max(1, total // 8)
+    rest = total - last
+    parts = 3
+    sizes = [rest // parts + (1 if i < rest % parts else 0) for i in range(parts)]
+    return sizes + [last]
+
+
+def exchange_and_square(total, operands):
+    x, y, picks, keys, rows, cols, slots, keep, send = operands
+    sizes = chunk_sizes(total)
+    swap = [(0, 1), (1, 0)]
+    arrived = []
+    first = 0
+    for size in sizes:
+        packed = pack_panels(y, picks[first : first + size])
+        arrived.append(lax.ppermute(packed, "rows", swap))
+        first += size
+    capacity = rows.shape[0]
+    dummy = keep.shape[0] - 1
+
+    def phase(panels, low, high, keep, send, apart):
+        begin = jnp.sum((keys < low).astype(jnp.int32))
+        steps = jnp.sum((keys < high).astype(jnp.int32)) - begin
+        live = steps > 0
+        roll = lambda v: lax.dynamic_slice(jnp.concatenate([v, v]), (begin,), (capacity,))
+        here_cols = roll(cols) - (low if apart else 0)
+        here_cols = jnp.where(live, here_cols, 0)
+        here_cols = jnp.clip(here_cols, 0, (high - low - 1) if apart else y.shape[2] // TILE - 1)
+        here_slots = jnp.where(live, roll(slots), dummy)
+        return square_slots(
+            x, panels, jnp.maximum(steps, 1), roll(rows), here_cols, here_slots, keep, send, apart
+        )
+
+    keep, send = phase(y, -1, 0, keep, send, False)
+    first = 0
+    for size, panels in zip(sizes, arrived):
+        keep, send = phase(panels, first, first + size, keep, send, True)
+        first += size
+    return keep, send
+
+
+def on_pair(x_act, grad_out, surv_rows, surv_cols, counts):
+    own_tiles = grad_out.shape[2] // TILE
+    capacity = surv_rows.shape[2]
+    row_place = lax.axis_index("rows")
+    slot_ids = jnp.arange(capacity, dtype=jnp.int32)
+    live = slot_ids < counts[0, 0]
+    listed = jnp.where(live, surv_cols[0, 0], -1)
+    axes = ("groups", "tiles", "rows")
+    everyone = lax.all_gather(listed, axes, axis=0, tiled=False)
+    columns = jnp.arange(2 * own_tiles, dtype=jnp.int32)
+    needed = jnp.any(everyone[:, None, :] == columns[None, :, None], axis=2)
+    owner_rows = (jnp.arange(everyone.shape[0], dtype=jnp.int32) % 2)[:, None]
+    remote = needed & ((columns // own_tiles)[None, :] != owner_rows)
+    largest = jnp.max(jnp.sum(remote.astype(jnp.int32), axis=1))
+
+    me = (lax.axis_index("groups") * lax.axis_size("tiles") + lax.axis_index("tiles")) * 2 + row_place
+
+    def places(owner, holder):
+        wanted = lax.dynamic_slice(remote, (owner, holder * own_tiles), (1, own_tiles))[0]
+        wanted = wanted.astype(jnp.int32)
+        ids = jnp.arange(own_tiles, dtype=jnp.int32)
+        before = jnp.sum(jnp.where(ids[None, :] < ids[:, None], wanted[None, :], 0), axis=1)
+        return wanted, before
+
+    ids = jnp.arange(own_tiles, dtype=jnp.int32)
+    partner = me + 1 - 2 * row_place
+    wanted, before = places(partner, row_place)
+    picks = jnp.sum(
+        jnp.where((wanted[None, :] > 0) & (before[None, :] == ids[:, None]), ids[None, :], 0), axis=1
+    )
+    _, arrival = places(me, 1 - row_place)
+    within = listed % own_tiles
+    is_local = listed // own_tiles == row_place
+    place = jnp.sum(jnp.where(within[:, None] == ids[None, :], arrival[None, :], 0), axis=1)
+    key = jnp.where(live, jnp.where(is_local, -1, place), 2 * own_tiles)
+    ahead = (key[None, :] < key[:, None]) | (
+        (key[None, :] == key[:, None]) & (slot_ids[None, :] < slot_ids[:, None])
+    )
+    rank = jnp.sum(ahead.astype(jnp.int32), axis=1)
+    chosen = rank[None, :] == slot_ids[:, None]
+    ordered = lambda v: jnp.sum(jnp.where(chosen, v[None, :], 0), axis=1)
+    keys = ordered(key)
+    rows = ordered(surv_rows[0, 0])
+    cols = ordered(jnp.where(is_local, within, place))
+    slots = ordered(slot_ids)
+
+    half = TILE // 2
+    keep = jnp.zeros((capacity + 1, half, TILE), jnp.float32)
+    send = jnp.zeros((capacity + 1, half, TILE), jnp.float32)
+    totals = sorted({max(4, own_tiles * n // 28) for n in TOTALS} | {own_tiles})
+    branch = jnp.sum((largest > jnp.array(totals[:-1], jnp.int32)).astype(jnp.int32))
+    operands = (x_act, grad_out, picks, keys, rows, cols, slots, keep, send)
+    keep, send = lax.switch(
+        branch, [functools.partial(exchange_and_square, total) for total in totals], operands
+    )
+    other = lax.ppermute(send, "tok", [(0, 1), (1, 0)])
+    return (keep + other)[:capacity][None, None]
+
+
+TOTALS = (12, 16, 18, 20, 22, 24, 28)
+
+
 def solution(mesh):
+    return functools.partial(choose, mesh)
+
+
+def choose(mesh, x_act, grad_out, surv_rows, surv_cols, counts):
+    own_columns = grad_out.shape[2] // (mesh.shape["tiles"] * mesh.shape["rows"])
+    paired = (
+        mesh.shape["rows"] == 2
+        and mesh.shape["tok"] == 2
+        and own_columns % TILE == 0
+        and own_columns // TILE >= 4
+    )
+    return spread(mesh, on_pair if paired else on_device)(
+        x_act, grad_out, surv_rows, surv_cols, counts
+    )
+
+
+def spread(mesh, body):
     return jax.shard_map(
-        on_device,
+        body,
         mesh=mesh,
         in_specs=(
             P("tok", "groups", "rows"),

time: 469 us -> 162 us (0.35)
  waiting for transfers between devices: 153 us -> 5.38 us
  blocking collectives: 146 us -> 42.2 us
  local copies, waits for them, and re-layouts: 109 us -> 8.73 us
  Pallas kernels: 0 us -> 69.8 us
  matrix products: 17.4 us -> 0 us
  loops' own time: 0.1 us -> 15.8 us
  between operations: 14.8 us -> 1.35 us
  starting transfers between devices: 9.92 us -> 4.09 us
    all_gather x1 -> x0, waiting for transfers between devices: 137 us -> none  [on_device(): gathered = lax.all_gather(grad_out, 'rows', axis=2, tiled=True)]
    unnamed x1 -> x0, blocking collectives: 137 us -> none
    pallas_call x0 -> x9, Pallas kernels: none -> 69.8 us  [the longest x5 52.5 us: square_slots(): pl.pallas_call(functools.partial(square_body, panels_apart), out_shape=(j...]
    gather x12 -> x0, local copies, waits for them, and re-layouts: 49.7 us -> none  [the longest x4 21.6 us: one_block(): x_panels = jnp.take(x_tiles, rows_here, axis=1)]
    all_gather x1, blocking collectives: 8.95 us -> 42.2 us  [on_pair(): everyone = lax.all_gather(listed, axes, axis=0, tiled=False)]
    while x2 -> x0, local copies, waits for them, and re-layouts: 23.3 us -> none  [square_tiles(): return lax.fori_loop(0, trip_count, one_block, result)]
    unnamed x12 -> x0, local copies, waits for them, and re-layouts: 18.8 us -> none
    dot_general x4 -> x0, matrix products: 17.4 us -> none  [one_block(): jnp.einsum('tnk,tnj->nkj', x_panels, y_panels, preferred_element_type=jnp...]
  transfers between devices with their start and end apart: 4 -> 5, of which waited for: 3 -> 2; matrix products, arithmetic and copies ran while one was open for 13% -> 5% of each run, Pallas kernels for 0% -> 39%
where the time goes in v1:
time: 162 us; the launch traced here: 159 us
  Pallas kernels  69.8 us (43%)
  blocking collectives  42.2 us (26%)
  loops' own time  15.8 us (10%)
  other arithmetic  12.1 us (7%)
  local copies, waits for them, and re-layouts  8.73 us (5%)
  waiting for transfers between devices  5.38 us (3%)
  starting transfers between devices  4.09 us (3%)
    pallas_call x5, Pallas kernels, square_slots(): pl.pallas_call(functools.partial(square_body, panels_apart), out_shape=(j...  52.5 us
    all_gather x1, blocking collectives, on_pair(): everyone = lax.all_gather(listed, axes, axis=0, tiled=False)  42.2 us
    pallas_call x4, Pallas kernels, pack_panels(): pl.pallas_call(pack_body, out_shape=jax.ShapeDtypeStruct((chosen, tokens,...  17.3 us
    another operation x1, loops' own time, on_pair(): lax.switch(branch, [functools.partial(exchange_and_square, total) for tot...  15.8 us
    ppermute x1, waiting for transfers between devices, on_pair(): other = lax.ppermute(send, 'tok', [(0, 1), (1, 0)])  4.41 us
    ppermute x4, starting transfers between devices, exchange_and_square(): arrived.append(lax.ppermute(packed, 'rows', swap))  4.09 us
    broadcast_in_dim x1, other arithmetic, on_pair(): return (keep + other)[:capacity][None, None]  3.3 us
  transfers between devices with their start and end apart: 5, of which 2 were waited for; matrix products, arithmetic and copies ran while one was open for 5% of the time, Pallas kernels for 39%

profile of v1, /device:TPU:0, one launch (start us, length us, event | category | flops | bytes accessed | tf_op | source)
XLA Modules:
  0.0 159.4 jit_solution(10363160270331229241)
XLA Ops:
  1.3 42.2 %all-gather = s32[16,1,64]{2,1,0:T(1,128)S(1)} all-gather(s32[1,1,64]{2,1,0:T(1,128)S(1)} %fusion.83), channel_id=1, replica_groups=mesh['groups'=2,'tiles'=4,'rows'=2,'tok'=2] {'groups','tiles','rows'}, dimensions={0}, use_global_device_ids=true | all-gather | bytes 4352 | tf_op jit(solution)/shard_map/all_gather | solution.py:234
  46.6 2.0 %fusion.84 = s32[]{:T(128)} fusion(s32[6]{0:T(128)} %constant.301.clone, s32[]{:T(128)} %reduce_max.9), kind=kLoop, calls=%fused_computation.251 | loop fusion | flops 17 | bytes 32 | tf_op jit(solution)/shard_map/reduce_sum | solution.py:276
  49.3 0.8 select_reduce_fusion
  50.1 101.6 %conditional.1 = ((f32[65,64,128]{2,1,0:T(8,128)}, f32[65,64,128]{2,1,0:T(8,128)})) conditional(s32[]{:T(128)} %clamp.37, (s32[64]{0:T(128)S(1)}, s32[64]{0:T(128)S(1)}, s32[64]{0:T(128)S(1)}, s32[64]{0:T(128)S(1)}, s32[28]{0:T(128)S(1)}, /*index=5*/bf16[1,768,3584]{2,1,0:T(8,128)(2,1)}, ...), branch_computations={%region_13.20_spmd, %region_20.27_spmd, %region_27.34_spmd, %regio... | conditional | flops 1610615552 | bytes 80032616 | solution.py:278
  51.0 5.6 %pack_panels.47 = bf16[7,768,128]{2,1,0:T(8,128)(2,1)} custom-call(s32[7]{0:T(128)} %get-tuple-element.354.pick_ref, bf16[1,768,3584]{2,1,0:T(8,128)(2,1)} %get-tuple-element.169.y_ref), custom_call_target="tpu_custom_call" | custom-call | bytes 2752512 | tf_op jit(solution)/shard_map/cond/branch_4_fun/pack_panels/pallas_call | solution.py:110
  56.6 5.6 %pack_panels.46 = bf16[7,768,128]{2,1,0:T(8,128)(2,1)} custom-call(s32[7]{0:T(128)} %get-tuple-element.355.pick_ref, bf16[1,768,3584]{2,1,0:T(8,128)(2,1)} %get-tuple-element.169.y_ref), custom_call_target="tpu_custom_call" | custom-call | bytes 2752512 | tf_op jit(solution)/shard_map/cond/branch_4_fun/pack_panels/pallas_call | solution.py:110
  62.2 2.0 %collective-permute-start.18 = (bf16[7,768,128]{2,1,0:T(8,128)(2,1)}, bf16[7,768,128]{2,1,0:T(8,128)(2,1)S(1)}, u32[]{:S(2)}, u32[]{:S(2)}) collective-permute-start(bf16[7,768,128]{2,1,0:T(8,128)(2,1)} %pack_panels.46), channel_id=1, source_target_pairs={{0,2},{2,0},{1,3},{3,1},{4,6},{6,4},{5,7},{7,5},{8,10},{10,8},{9,1... | collective-permute-start | bytes 4128776 | tf_op jit(solution)/shard_map/cond/branch_4_fun/ppermute | solution.py:200
  64.8 3.8 %pack_panels.45 = bf16[6,768,128]{2,1,0:T(8,128)(2,1)} custom-call(s32[6]{0:T(128)} %slice.75.pick_ref, bf16[1,768,3584]{2,1,0:T(8,128)(2,1)} %get-tuple-element.169.y_ref), custom_call_target="tpu_custom_call" | custom-call | bytes 2359296 | tf_op jit(solution)/shard_map/cond/branch_4_fun/pack_panels/pallas_call | solution.py:110
  68.6 1.3 collective-permute-start.17
  70.6 2.4 %pack_panels.44 = bf16[2,768,128]{2,1,0:T(8,128)(2,1)} custom-call(s32[2]{0:T(128)} %slice.74.pick_ref, bf16[1,768,3584]{2,1,0:T(8,128)(2,1)} %get-tuple-element.169.y_ref), custom_call_target="tpu_custom_call" | custom-call | bytes 786432 | tf_op jit(solution)/shard_map/cond/branch_4_fun/pack_panels/pallas_call | solution.py:110
  72.9 0.8 collective-permute-start.16
  92.1 1.6 %broadcast_72_a_ref_b_ref.0.a_ref = f32[65,64,128]{2,1,0:T(8,128)} broadcast(f32[]{:T(128)} %constant.252.clone), dimensions={} | broadcast | bytes 2129924 | tf_op jit(solution)/shard_map/broadcast.72.a_ref.b_ref | solution.py:300
  93.7 1.6 broadcast_72_a_ref_b_ref.0.clone.b_ref
  95.3 22.4 %square_slots.55 = (f32[65,64,128]{2,1,0:T(8,128)}, f32[65,64,128]{2,1,0:T(8,128)}) custom-call(s32[1]{0:T(128)} %bitcast.24.steps_ref, s32[64]{0:T(128)} %get-tuple-element.349.rows_ref, s32[64]{0:T(128)} %get-tuple-element.344.cols_ref, s32[64]{0:T(128)} %get-tuple-element.339.slots_ref, ...), custom_call_target="tpu_custom_call", output_to_operand_aliasing={{0}: (6, {}), {1}: (7, {})} | custom-call | flops 805306368 | bytes 14680064 | tf_op jit(solution)/shard_map/cond/branch_4_fun/square_slots/pallas_call | solution.py:166
  117.7 1.1 copy-done.5
  118.8 11.1 %square_slots.56 = (f32[65,64,128]{2,1,0:T(8,128)}, f32[65,64,128]{2,1,0:T(8,128)}) custom-call(s32[1]{0:T(128)} %bitcast.23.steps_ref, s32[64]{0:T(128)} %get-tuple-element.350.rows_ref, s32[64]{0:T(128)} %get-tuple-element.345.cols_ref, s32[64]{0:T(128)} %get-tuple-element.340.slots_ref, ...), custom_call_target="tpu_custom_call", output_to_operand_aliasing={{0}: (6, {}), {1}: (7, {})} | custom-call | flops 201326592 | bytes 3670016 | tf_op jit(solution)/shard_map/cond/branch_4_fun/square_slots/pallas_call | solution.py:166
  129.9 1.1 copy-done.3
  131.0 8.6 %square_slots.57 = (f32[65,64,128]{2,1,0:T(8,128)}, f32[65,64,128]{2,1,0:T(8,128)}) custom-call(s32[1]{0:T(128)} %bitcast.22.steps_ref, s32[64]{0:T(128)} %get-tuple-element.351.rows_ref, s32[64]{0:T(128)} %get-tuple-element.346.cols_ref, s32[64]{0:T(128)} %get-tuple-element.341.slots_ref, ...), custom_call_target="tpu_custom_call", output_to_operand_aliasing={{0}: (6, {}), {1}: (7, {})} | custom-call | flops 201326592 | bytes 3670016 | tf_op jit(solution)/shard_map/cond/branch_4_fun/square_slots/pallas_call | solution.py:166
  139.6 1.0 collective-permute-done.17.y_ref
  140.6 7.8 %square_slots.58 = (f32[65,64,128]{2,1,0:T(8,128)}, f32[65,64,128]{2,1,0:T(8,128)}) custom-call(s32[1]{0:T(128)} %bitcast.21.steps_ref, s32[64]{0:T(128)} %get-tuple-element.352.rows_ref, s32[64]{0:T(128)} %get-tuple-element.347.cols_ref, s32[64]{0:T(128)} %get-tuple-element.342.slots_ref, ...), custom_call_target="tpu_custom_call", output_to_operand_aliasing={{0}: (6, {}), {1}: (7, {})} | custom-call | flops 201326592 | bytes 3670016 | tf_op jit(solution)/shard_map/cond/branch_4_fun/square_slots/pallas_call | solution.py:166
  148.3 0.7 copy-done.21
  149.1 2.6 %square_slots.59 = (f32[65,64,128]{2,1,0:T(8,128)}, f32[65,64,128]{2,1,0:T(8,128)}) custom-call(s32[1]{0:T(128)} %bitcast.20.steps_ref, s32[64]{0:T(128)} %get-tuple-element.353.rows_ref, s32[64]{0:T(128)} %get-tuple-element.348.cols_ref, s32[64]{0:T(128)} %get-tuple-element.343.slots_ref, ...), custom_call_target="tpu_custom_call", output_to_operand_aliasing={{0}: (6, {}), {1}: (7, {})} | custom-call | flops 201326592 | bytes 3670016 | tf_op jit(solution)/shard_map/cond/branch_4_fun/square_slots/pallas_call | solution.py:166
  151.7 4.4 %collective-permute-done.28 = f32[65,64,128]{2,1,0:T(8,128)S(1)} collective-permute-done((f32[65,64,128]{2,1,0:T(8,128)}, f32[65,64,128]{2,1,0:T(8,128)S(1)}, u32[]{:S(2)}, u32[]{:S(2)}) %collective-permute-start.28) | collective-permute-done | bytes 2129952 | tf_op jit(solution)/shard_map/ppermute | solution.py:281
  156.1 3.3 %fusion.78 = f32[1,1,64,64,128]{4,3,2,1,0:T(8,128)} fusion(f32[65,64,128]{2,1,0:T(8,128)S(1)} %collective-permute-done.28, f32[65,64,128]{2,1,0:T(8,128)} %get-tuple-element.210), kind=kLoop, calls=%fused_computation.212 | loop fusion | flops 524288 | bytes 6291456 | tf_op jit(solution)/shard_map/broadcast_in_dim | solution.py:282
  (31 shorter events, 8.6 us)
Async XLA Ops:
  56.6 61.1 %collective-permute-start.19 = (bf16[7,768,128]{2,1,0:T(8,128)(2,1)}, bf16[7,768,128]{2,1,0:T(8,128)(2,1)S(1)}, u32[]{:S(2)}, u32[]{:S(2)}) collective-permute-start(bf16[7,768,128]{2,1,0:T(8,128)(2,1)} %pack_panels.47), channel_id=1, source_target_pairs={{0,2},{2,0},{1,3},{3,1},{4,6},{6,4},{5,7},{7,5},{8,10},{10,8},{9,1... | collective-permute-start | bytes 4128776 | tf_op jit(solution)/shard_map/cond/branch_4_fun/ppermute | solution.py:200
  62.2 67.7 %collective-permute-start.18 = (bf16[7,768,128]{2,1,0:T(8,128)(2,1)}, bf16[7,768,128]{2,1,0:T(8,128)(2,1)S(1)}, u32[]{:S(2)}, u32[]{:S(2)}) collective-permute-start(bf16[7,768,128]{2,1,0:T(8,128)(2,1)} %pack_panels.46), channel_id=1, source_target_pairs={{0,2},{2,0},{1,3},{3,1},{4,6},{6,4},{5,7},{7,5},{8,10},{10,8},{9,1... | collective-permute-start | bytes 4128776 | tf_op jit(solution)/shard_map/cond/branch_4_fun/ppermute | solution.py:200
  68.6 72.0 %collective-permute-start.17 = (bf16[6,768,128]{2,1,0:T(8,128)(2,1)}, bf16[6,768,128]{2,1,0:T(8,128)(2,1)}, u32[]{:S(2)}, u32[]{:S(2)}) collective-permute-start(bf16[6,768,128]{2,1,0:T(8,128)(2,1)} %pack_panels.45), channel_id=1, source_target_pairs={{0,2},{2,0},{1,3},{3,1},{4,6},{6,4},{5,7},{7,5},{8,10},{10,8},{9,1... | collective-permute-start | bytes 3538952 | tf_op jit(solution)/shard_map/cond/branch_4_fun/ppermute | solution.py:200
  72.9 75.4 %collective-permute-start.16 = (bf16[2,768,128]{2,1,0:T(8,128)(2,1)}, bf16[2,768,128]{2,1,0:T(8,128)(2,1)S(1)}, u32[]{:S(2)}, u32[]{:S(2)}) collective-permute-start(bf16[2,768,128]{2,1,0:T(8,128)(2,1)} %pack_panels.44), channel_id=1, source_target_pairs={{0,2},{2,0},{1,3},{3,1},{4,6},{6,4},{5,7},{7,5},{8,10},{10,8},{9,1... | collective-permute-start | bytes 1179656 | tf_op jit(solution)/shard_map/cond/branch_4_fun/ppermute | solution.py:200
  117.7 1.1 copy-start.5
  129.9 1.1 copy-start.3
  148.3 0.7 copy-start.21
  151.7 4.4 %collective-permute-start.28 = (f32[65,64,128]{2,1,0:T(8,128)}, f32[65,64,128]{2,1,0:T(8,128)S(1)}, u32[]{:S(2)}, u32[]{:S(2)}) collective-permute-start(f32[65,64,128]{2,1,0:T(8,128)} %get-tuple-element.211), channel_id=1, source_target_pairs={{0,1},{1,0},{2,3},{3,2},{4,5},{5,4},{6,7},{7,6},{8,9},{9,8},{10,11... | collective-permute-start | bytes 6389768 | tf_op jit(solution)/shard_map/ppermute | solution.py:281

commit v2 on v1

--- a/solution.py
+++ b/solution.py
@@ -100,8 +100,78 @@
     return fisher[None, None]
 
 
-def pack_body(pick_ref, y_ref, out_ref):
-    out_ref[...] = y_ref[...]
+def share_body(listed_ref, all_ref, send_sems, recv_sems, own_sem):
+    tiles, row_count = lax.axis_size("tiles"), lax.axis_size("rows")
+    owners = all_ref.shape[0]
+    me = (
+        lax.axis_index("groups") * tiles + lax.axis_index("tiles")
+    ) * row_count + lax.axis_index("rows")
+
+    def peer(step):
+        there = lax.rem(me + step, owners)
+        return {
+            "groups": there // (tiles * row_count),
+            "tiles": lax.rem(there // row_count, tiles),
+            "rows": lax.rem(there, row_count),
+        }
+
+    barrier = pltpu.get_barrier_semaphore()
+    for step in range(1, owners):
+        pl.semaphore_signal(
+            barrier, inc=1, device_id=peer(step), device_id_type=pl.DeviceIdType.MESH
+        )
+    pl.semaphore_wait(barrier, owners - 1)
+    own = pltpu.make_async_copy(listed_ref, all_ref.at[me], own_sem)
+    own.start()
+    copies = []
+    for step in range(1, owners):
+        copy = pltpu.make_async_remote_copy(
+            src_ref=listed_ref,
+            dst_ref=all_ref.at[me],
+            send_sem=send_sems.at[step],
+            recv_sem=recv_sems.at[step],
+            device_id=peer(step),
+            device_id_type=pl.DeviceIdType.MESH,
+        )
+        copy.start()
+        copies.append(copy)
+    own.wait()
+    for copy in copies:
+        copy.wait()
+
+
+def share_lists(listed):
+    owners = lax.axis_size("groups") * lax.axis_size("tiles") * lax.axis_size("rows")
+    capacity = listed.shape[0]
+    lanes = -(-capacity // 128) * 128
+    row = jnp.broadcast_to(jnp.pad(listed, (0, lanes - capacity))[None, :], (8, lanes))
+    shared = pl.pallas_call(
+        share_body,
+        out_shape=jax.ShapeDtypeStruct((owners, 8, lanes), jnp.int32),
+        in_specs=[pl.BlockSpec(memory_space=pltpu.VMEM)],
+        out_specs=pl.BlockSpec(memory_space=pltpu.VMEM),
+        scratch_shapes=[
+            pltpu.SemaphoreType.DMA((owners,)),
+            pltpu.SemaphoreType.DMA((owners,)),
+            pltpu.SemaphoreType.DMA,
+        ],
+        compiler_params=pltpu.CompilerParams(collective_id=3, has_side_effects=True),
+        name="share_lists",
+    )(row)
+    return shared[:, 0, :capacity]
+
+
+def pack_body(pick_ref, y_ref, out_ref, sems):
+    copies = []
+    for i in range(out_ref.shape[0]):
+        first = pl.multiple_of(pick_ref[i] * TILE, TILE)
+        copy = pltpu.make_async_copy(
+            y_ref.at[0, :, pl.ds(first, TILE)], out_ref.at[i], sems.at[i]
+        )
+        copy.start()
+        copies.append(copy)
+    for copy in copies:
+        copy.wait()
 
 
 def pack_panels(y, picks):
@@ -110,12 +180,9 @@
     return pl.pallas_call(
         pack_body,
         out_shape=jax.ShapeDtypeStruct((chosen, tokens, TILE), y.dtype),
-        grid_spec=pltpu.PrefetchScalarGridSpec(
-            num_scalar_prefetch=1,
-            grid=(chosen,),
-            in_specs=[pl.BlockSpec((1, tokens, TILE), lambda i, p: (0, 0, p[i]))],
-            out_specs=pl.BlockSpec((1, tokens, TILE), lambda i, p: (i, 0, 0)),
-        ),
+        in_specs=[pl.BlockSpec(memory_space=pltpu.SMEM), pl.BlockSpec(memory_space=pl.ANY)],
+        out_specs=pl.BlockSpec(memory_space=pl.ANY),
+        scratch_shapes=[pltpu.SemaphoreType.DMA((chosen,))],
         cost_estimate=pl.CostEstimate(
             flops=0, bytes_accessed=4 * chosen * tokens * TILE, transcendentals=0
         ),
@@ -230,8 +297,7 @@
     slot_ids = jnp.arange(capacity, dtype=jnp.int32)
     live = slot_ids < counts[0, 0]
     listed = jnp.where(live, surv_cols[0, 0], -1)
-    axes = ("groups", "tiles", "rows")
-    everyone = lax.all_gather(listed, axes, axis=0, tiled=False)
+    everyone = share_lists(listed)
     columns = jnp.arange(2 * own_tiles, dtype=jnp.int32)
     needed = jnp.any(everyone[:, None, :] == columns[None, :, None], axis=2)
     owner_rows = (jnp.arange(everyone.shape[0], dtype=jnp.int32) % 2)[:, None]
@@ -282,7 +348,7 @@
     return (keep + other)[:capacity][None, None]
 
 
-TOTALS = (12, 16, 18, 20, 22, 24, 28)
+TOTALS = (8, 12, 14, 15, 16, 17, 18, 19, 20, 21, 22, 23, 24, 26, 28)
 
 
 def solution(mesh):

time: 162 us -> 250 us (1.54)
  the two profiles are of different devices: /device:TPU:0 before, /device:TPU:13 now
where the time goes in v2:
time: 250 us; the launch traced here: 248 us
  Pallas kernels  200 us (80%)
  loops' own time  15.9 us (6%)
  other arithmetic  10.8 us (4%)
  local copies, waits for them, and re-layouts  10.2 us (4%)
  starting transfers between devices  5.89 us (2%)
  waiting for transfers between devices  4.05 us (2%)
    pallas_call x4, Pallas kernels, pack_panels(): pl.pallas_call(pack_body, out_shape=jax.ShapeDtypeStruct((chosen, tokens,...  138 us
    pallas_call x5, Pallas kernels, square_slots(): pl.pallas_call(functools.partial(square_body, panels_apart), out_shape=(j...  53.1 us
    another operation x1, loops' own time, on_pair(): lax.switch(branch, [functools.partial(exchange_and_square, total) for tot...  15.9 us
    pallas_call x1, Pallas kernels, share_lists(): pl.pallas_call(share_body, out_shape=jax.ShapeDtypeStruct((owners, 8, lan...  8.49 us
  transfers between devices with their start and end apart: 5, of which 1 were waited for; matrix products, arithmetic and copies ran while one was open for 3% of the time, Pallas kernels for 59%

profile of v2, /device:TPU:13, one launch (start us, length us, event | category | flops | bytes accessed | tf_op | source)
XLA Modules:
  0.0 248.0 jit_solution(12281767775517395084)
XLA Ops:
  1.9 8.5 %share_lists.1 = s32[16,8,128]{2,1,0:T(8,128)} custom-call(s32[8,128]{1,0:T(8,128)} %broadcast_in_dim.296.listed_ref), custom_call_target="tpu_custom_call" | custom-call | tf_op jit(solution)/shard_map/share_lists/pallas_call | solution.py:148
  10.4 0.8 slice.186
  13.1 2.0 fusion.174
  15.8 0.8 select_reduce_fusion
  16.6 221.4 %conditional.1 = ((f32[65,64,128]{2,1,0:T(8,128)}, f32[65,64,128]{2,1,0:T(8,128)})) conditional(s32[]{:T(128)} %clamp.74, (s32[64]{0:T(128)S(1)}, s32[64]{0:T(128)S(1)}, s32[64]{0:T(128)S(1)}, s32[64]{0:T(128)S(1)}, s32[28]{0:T(128)S(1)}, /*index=5*/bf16[1,768,3584]{2,1,0:T(8,128)(2,1)}, ...), branch_computations={%region_13.20_spmd, %region_20.27_spmd, %region_27.34_spmd, %regio... | conditional | flops 1610615552 | bytes 80030504 | solution.py:344
  17.5 43.5 %pack_panels.103 = bf16[7,768,128]{2,1,0:T(8,128)(2,1)} custom-call(s32[7]{0:T(128)} %get-tuple-element.751.pick_ref, bf16[1,768,3584]{2,1,0:T(8,128)(2,1)} %get-tuple-element.371.y_ref), custom_call_target="tpu_custom_call" | custom-call | bytes 2752512 | tf_op jit(solution)/shard_map/cond/branch_10_fun/pack_panels/pallas_call | solution.py:180
  61.0 1.3 collective-permute-start.43
  62.3 43.5 %pack_panels.102 = bf16[7,768,128]{2,1,0:T(8,128)(2,1)} custom-call(s32[7]{0:T(128)} %get-tuple-element.752.pick_ref, bf16[1,768,3584]{2,1,0:T(8,128)(2,1)} %get-tuple-element.371.y_ref), custom_call_target="tpu_custom_call" | custom-call | bytes 2752512 | tf_op jit(solution)/shard_map/cond/branch_10_fun/pack_panels/pallas_call | solution.py:180
  106.8 37.6 %pack_panels.101 = bf16[6,768,128]{2,1,0:T(8,128)(2,1)} custom-call(s32[6]{0:T(128)} %slice.165.pick_ref, bf16[1,768,3584]{2,1,0:T(8,128)(2,1)} %get-tuple-element.371.y_ref), custom_call_target="tpu_custom_call" | custom-call | bytes 2359296 | tf_op jit(solution)/shard_map/cond/branch_10_fun/pack_panels/pallas_call | solution.py:180
  144.4 1.3 collective-permute-start.41
  146.3 13.7 %pack_panels.100 = bf16[2,768,128]{2,1,0:T(8,128)(2,1)} custom-call(s32[2]{0:T(128)} %slice.164.pick_ref, bf16[1,768,3584]{2,1,0:T(8,128)(2,1)} %get-tuple-element.371.y_ref), custom_call_target="tpu_custom_call" | custom-call | bytes 786432 | tf_op jit(solution)/shard_map/cond/branch_10_fun/pack_panels/pallas_call | solution.py:180
  178.8 1.6 broadcast_156_a_ref_b_ref.0.a_ref
  180.4 1.6 broadcast_156_a_ref_b_ref.0.clone.b_ref
  181.9 28.6 %square_slots.125 = (f32[65,64,128]{2,1,0:T(8,128)}, f32[65,64,128]{2,1,0:T(8,128)}) custom-call(s32[1]{0:T(128)} %bitcast.54.steps_ref, s32[64]{0:T(128)} %get-tuple-element.746.rows_ref, s32[64]{0:T(128)} %get-tuple-element.741.cols_ref, s32[64]{0:T(128)} %get-tuple-element.736.slots_ref, ...), custom_call_target="tpu_custom_call", output_to_operand_aliasing={{0}: (6, {}), {1}: (7, {})} | custom-call | flops 805306368 | bytes 14680064 | tf_op jit(solution)/shard_map/cond/branch_10_fun/square_slots/pallas_call | solution.py:233
  210.5 1.1 copy-done.10
  211.6 8.6 %square_slots.126 = (f32[65,64,128]{2,1,0:T(8,128)}, f32[65,64,128]{2,1,0:T(8,128)}) custom-call(s32[1]{0:T(128)} %bitcast.53.steps_ref, s32[64]{0:T(128)} %get-tuple-element.747.rows_ref, s32[64]{0:T(128)} %get-tuple-element.742.cols_ref, s32[64]{0:T(128)} %get-tuple-element.737.slots_ref, ...), custom_call_target="tpu_custom_call", output_to_operand_aliasing={{0}: (6, {}), {1}: (7, {})} | custom-call | flops 201326592 | bytes 3670016 | tf_op jit(solution)/shard_map/cond/branch_10_fun/square_slots/pallas_call | solution.py:233
  220.2 1.1 copy-done.6
  221.3 10.4 %square_slots.127 = (f32[65,64,128]{2,1,0:T(8,128)}, f32[65,64,128]{2,1,0:T(8,128)}) custom-call(s32[1]{0:T(128)} %bitcast.52.steps_ref, s32[64]{0:T(128)} %get-tuple-element.748.rows_ref, s32[64]{0:T(128)} %get-tuple-element.743.cols_ref, s32[64]{0:T(128)} %get-tuple-element.738.slots_ref, ...), custom_call_target="tpu_custom_call", output_to_operand_aliasing={{0}: (6, {}), {1}: (7, {})} | custom-call | flops 201326592 | bytes 3670016 | tf_op jit(solution)/shard_map/cond/branch_10_fun/square_slots/pallas_call | solution.py:233
  231.7 2.9 %square_slots.128 = (f32[65,64,128]{2,1,0:T(8,128)}, f32[65,64,128]{2,1,0:T(8,128)}) custom-call(s32[1]{0:T(128)} %bitcast.51.steps_ref, s32[64]{0:T(128)} %get-tuple-element.749.rows_ref, s32[64]{0:T(128)} %get-tuple-element.744.cols_ref, s32[64]{0:T(128)} %get-tuple-element.739.slots_ref, ...), custom_call_target="tpu_custom_call", output_to_operand_aliasing={{0}: (6, {}), {1}: (7, {})} | custom-call | flops 201326592 | bytes 3670016 | tf_op jit(solution)/shard_map/cond/branch_10_fun/square_slots/pallas_call | solution.py:233
  234.6 0.7 copy-done.42
  235.4 2.6 %square_slots.129 = (f32[65,64,128]{2,1,0:T(8,128)}, f32[65,64,128]{2,1,0:T(8,128)}) custom-call(s32[1]{0:T(128)} %bitcast.50.steps_ref, s32[64]{0:T(128)} %get-tuple-element.750.rows_ref, s32[64]{0:T(128)} %get-tuple-element.745.cols_ref, s32[64]{0:T(128)} %get-tuple-element.740.slots_ref, ...), custom_call_target="tpu_custom_call", output_to_operand_aliasing={{0}: (6, {}), {1}: (7, {})} | custom-call | flops 201326592 | bytes 3670016 | tf_op jit(solution)/shard_map/cond/branch_10_fun/square_slots/pallas_call | solution.py:233
  238.0 2.7 %collective-permute-start.60 = (f32[65,64,128]{2,1,0:T(8,128)}, f32[65,64,128]{2,1,0:T(8,128)S(1)}, u32[]{:S(2)}, u32[]{:S(2)}) collective-permute-start(f32[65,64,128]{2,1,0:T(8,128)} %get-tuple-element.443), channel_id=1, source_target_pairs={{0,1},{1,0},{2,3},{3,2},{4,5},{5,4},{6,7},{7,6},{8,9},{9,8},{10,11... | collective-permute-start | bytes 6389768 | tf_op jit(solution)/shard_map/ppermute | solution.py:347
  240.7 4.0 %collective-permute-done.60 = f32[65,64,128]{2,1,0:T(8,128)S(1)} collective-permute-done((f32[65,64,128]{2,1,0:T(8,128)}, f32[65,64,128]{2,1,0:T(8,128)S(1)}, u32[]{:S(2)}, u32[]{:S(2)}) %collective-permute-start.60) | collective-permute-done | bytes 2129952 | tf_op jit(solution)/shard_map/ppermute | solution.py:347
  244.7 3.3 %fusion.169 = f32[1,1,64,64,128]{4,3,2,1,0:T(8,128)} fusion(f32[65,64,128]{2,1,0:T(8,128)S(1)} %collective-permute-done.60, f32[65,64,128]{2,1,0:T(8,128)} %get-tuple-element.442), kind=kLoop, calls=%fused_computation.455 | loop fusion | flops 524288 | bytes 6291456 | tf_op jit(solution)/shard_map/broadcast_in_dim | solution.py:348
  (33 shorter events, 8.5 us)
Async XLA Ops:
  61.0 149.5 %collective-permute-start.43 = (bf16[7,768,128]{2,1,0:T(8,128)(2,1)}, bf16[7,768,128]{2,1,0:T(8,128)(2,1)S(1)}, u32[]{:S(2)}, u32[]{:S(2)}) collective-permute-start(bf16[7,768,128]{2,1,0:T(8,128)(2,1)} %pack_panels.103), channel_id=1, source_target_pairs={{0,2},{2,0},{1,3},{3,1},{4,6},{6,4},{5,7},{7,5},{8,10},{10,8},{9,1... | collective-permute-start | bytes 4128776 | tf_op jit(solution)/shard_map/cond/branch_10_fun/ppermute | solution.py:267
  105.9 114.3 %collective-permute-start.42 = (bf16[7,768,128]{2,1,0:T(8,128)(2,1)}, bf16[7,768,128]{2,1,0:T(8,128)(2,1)S(1)}, u32[]{:S(2)}, u32[]{:S(2)}) collective-permute-start(bf16[7,768,128]{2,1,0:T(8,128)(2,1)} %pack_panels.102), channel_id=1, source_target_pairs={{0,2},{2,0},{1,3},{3,1},{4,6},{6,4},{5,7},{7,5},{8,10},{10,8},{9,1... | collective-permute-start | bytes 4128776 | tf_op jit(solution)/shard_map/cond/branch_10_fun/ppermute | solution.py:267
  144.4 87.3 %collective-permute-start.41 = (bf16[6,768,128]{2,1,0:T(8,128)(2,1)}, bf16[6,768,128]{2,1,0:T(8,128)(2,1)}, u32[]{:S(2)}, u32[]{:S(2)}) collective-permute-start(bf16[6,768,128]{2,1,0:T(8,128)(2,1)} %pack_panels.101), channel_id=1, source_target_pairs={{0,2},{2,0},{1,3},{3,1},{4,6},{6,4},{5,7},{7,5},{8,10},{10,8},{9,1... | collective-permute-start | bytes 3538952 | tf_op jit(solution)/shard_map/cond/branch_10_fun/ppermute | solution.py:267
  160.0 74.6 %collective-permute-start.40 = (bf16[2,768,128]{2,1,0:T(8,128)(2,1)}, bf16[2,768,128]{2,1,0:T(8,128)(2,1)S(1)}, u32[]{:S(2)}, u32[]{:S(2)}) collective-permute-start(bf16[2,768,128]{2,1,0:T(8,128)(2,1)} %pack_panels.100), channel_id=1, source_target_pairs={{0,2},{2,0},{1,3},{3,1},{4,6},{6,4},{5,7},{7,5},{8,10},{10,8},{9,1... | collective-permute-start | bytes 1179656 | tf_op jit(solution)/shard_map/cond/branch_10_fun/ppermute | solution.py:267
  210.5 1.1 copy-start.10
  220.2 1.1 copy-start.6
  234.6 0.7 copy-start.42
  238.0 6.7 %collective-permute-start.60 = (f32[65,64,128]{2,1,0:T(8,128)}, f32[65,64,128]{2,1,0:T(8,128)S(1)}, u32[]{:S(2)}, u32[]{:S(2)}) collective-permute-start(f32[65,64,128]{2,1,0:T(8,128)} %get-tuple-element.443), channel_id=1, source_target_pairs={{0,1},{1,0},{2,3},{3,2},{4,5},{5,4},{6,7},{7,6},{8,9},{9,8},{10,11... | collective-permute-start | bytes 6389768 | tf_op jit(solution)/shard_map/ppermute | solution.py:347
